TPU v7x, 32 devices: a whole 2x2x4 slice. The times are simulated.
32 devices in a mesh: dp: 8 (over z, x), section: 4 (over y, core).
Axes of the slice: x: 2, y: 2, z: 4, core: 2. Of those that a mesh axis runs over, the one named last changes fastest.
Arguments:
- images_in: bfloat16 [2048, 4096], P(('dp', 'section')), may hold values from -6 to 6
- labels: int32 [2048], P(('dp', 'section')), may hold values from 0 to 9
- conv_weight: float32 [3, 2, 576, 64], P(None, None, None, 'section'), may hold values from -0.25 to 0.25
- frn_gain: float32 [3, 2, 64], replicated, may hold values from 0.25 to 1.75
- frn_bias: float32 [3, 2, 64], replicated, may hold values from -3 to 3
- head_weight: float32 [64, 10], replicated, as said below
- head_bias: float32 [10], replicated, may hold values from -4 to 4
Outputs:
- grad_conv: float32 [3, 2, 576, 64], P(None, None, None, 'section')
- grad_norm: float32 [3, 2, 2, 64], replicated
- grad_head_weight: float32 [64, 10], replicated
- grad_head_bias: float32 [10], replicated
Inputs may be any that keep to these rules, and one draw needn't show every extreme that they name: `head_weight`: the classifier's weights.
All inputs are finite; a program needn't handle non-finite values.
Results may differ from a plain program's by a relative error of at most 0.0033.
The roundings to bfloat16 on the way count: a program that leaves them out, or rounds other values in their place, can miss the bound.
Values may be sent and summed in bfloat16 or wider, within the bound.
A program may use at most 64 MiB of HBM per device.

v0:
```python
import jax
import jax.numpy as jnp
from jax import lax
from jax.sharding import PartitionSpec as P

SIDE = 8
MICRO = 8
eps = 1e-06
prior_precision = 0.5


def make_patches(maps):
    side = maps.shape[1]
    padded = jnp.pad(maps, ((0, 0), (1, 1), (1, 1), (0, 0)))
    taps = [padded[:, a : a + side, e : e + side, :] for a in range(3) for e in range(3)]
    stacked = jnp.concatenate(taps, axis=3)
    return stacked.reshape(maps.shape[0] * side * side, 9 * maps.shape[3])


def fold_patches(columns, shape):
    back = jax.vjp(make_patches, jnp.zeros(shape, jnp.float32))[1]
    return back(columns)[0]


def respond(values, gain, bias, count):
    grouped = values.reshape(count, -1, values.shape[1])
    energy = jnp.mean(grouped * grouped, axis=1, keepdims=True)
    normed = grouped * lax.rsqrt(energy + eps)
    return (gain * normed + bias).reshape(values.shape)


def swish(values):
    return values * jax.nn.sigmoid(values)


def block_forward(maps, weights, gains, biases):
    count = maps.shape[0]
    w_first = weights[0]
    w_second = weights[1]
    cols_first = make_patches(maps)
    pre_first = jnp.dot(cols_first, w_first, preferred_element_type=jnp.float32)
    hidden = swish(respond(pre_first, gains[0], biases[0], count)).astype(jnp.bfloat16)
    cols_second = make_patches(hidden.reshape(maps.shape))
    pre_second = jnp.dot(cols_second, w_second, preferred_element_type=jnp.float32)
    skip = maps.reshape(pre_second.shape).astype(jnp.float32)
    result = swish(skip + respond(pre_second, gains[1], biases[1], count)).astype(jnp.bfloat16)
    return (result.reshape(maps.shape), (cols_first, pre_first, cols_second, pre_second))


def block_backward(maps, cotangent, weights, gains, biases):
    count = maps.shape[0]
    w_first = weights[0]
    w_second = weights[1]
    saved = block_forward(maps, weights, gains, biases)[1]
    cols_first, pre_first, cols_second, pre_second = saved

    def second_part(values, skip, gain, bias):
        return swish(skip + respond(values, gain, bias, count))

    def first_part(values, gain, bias):
        return swish(respond(values, gain, bias, count))

    skip = maps.reshape(pre_second.shape).astype(jnp.float32)
    back_second = jax.vjp(second_part, pre_second, skip, gains[1], biases[1])[1]
    d_second, d_skip, dg_second, db_second = back_second(
        cotangent.reshape(pre_second.shape).astype(jnp.float32)
    )
    q_second = d_second.astype(jnp.bfloat16)
    dw_second = jnp.dot(cols_second.T, q_second, preferred_element_type=jnp.float32)
    d_hidden = fold_patches(
        jnp.dot(q_second, w_second.T, preferred_element_type=jnp.float32), maps.shape
    )
    back_first = jax.vjp(first_part, pre_first, gains[0], biases[0])[1]
    d_first, dg_first, db_first = back_first(d_hidden.reshape(pre_first.shape))
    q_first = d_first.astype(jnp.bfloat16)
    dw_first = jnp.dot(cols_first.T, q_first, preferred_element_type=jnp.float32)
    d_input = fold_patches(
        jnp.dot(q_first, w_first.T, preferred_element_type=jnp.float32), maps.shape
    )
    d_maps = (d_skip.reshape(maps.shape) + d_input).astype(jnp.bfloat16)
    d_norm = jnp.stack([jnp.stack([dg_first, db_first]), jnp.stack([dg_second, db_second])])
    return (d_maps, jnp.stack([dw_first, dw_second]), d_norm)


def head_grads(final, labels, head_w, head_b, total):
    count = final.shape[0]
    width = final.shape[3]
    pixels = final.shape[1] * final.shape[2]
    pooled = jnp.mean(final.reshape(count, pixels, width).astype(jnp.float32), axis=1)
    logits = jnp.dot(pooled, head_w, precision=lax.Precision.HIGHEST) + head_b
    top = jnp.max(logits, axis=1, keepdims=True)
    expo = jnp.exp(logits - top)
    probs = expo / jnp.sum(expo, axis=1, keepdims=True)
    onehot = (labels[:, None] == jnp.arange(head_w.shape[1])[None, :]).astype(jnp.float32)
    d_logits = (probs - onehot) / total
    d_head_w = jnp.dot(pooled.T, d_logits, precision=lax.Precision.HIGHEST)
    d_head_b = jnp.sum(d_logits, axis=0)
    d_pooled = jnp.dot(d_logits, head_w.T, precision=lax.Precision.HIGHEST) / pixels
    spread = jnp.broadcast_to(d_pooled[:, None, :], (count, pixels, width))
    return (spread.astype(jnp.bfloat16).reshape(final.shape), d_head_w, d_head_b)


def group_grads(maps, labels, weights, gains, biases, head_w, head_b, total):
    saved = []
    for index in range(weights.shape[0]):
        saved.append(maps)
        maps = block_forward(maps, weights[index], gains[index], biases[index])[0]
    cotangent, d_head_w, d_head_b = head_grads(maps, labels, head_w, head_b, total)
    conv_terms = []
    norm_terms = []
    for index in reversed(range(weights.shape[0])):
        cotangent, d_conv, d_norm = block_backward(
            saved[index], cotangent, weights[index], gains[index], biases[index]
        )
        conv_terms.insert(0, d_conv)
        norm_terms.insert(0, d_norm)
    return (jnp.stack(conv_terms), jnp.stack(norm_terms), d_head_w, d_head_b)


def accumulate(maps, labels, weights, gains, biases, head_w, head_b, total):
    width = weights.shape[3]
    initial = (
        jnp.zeros(weights.shape, jnp.float32),
        jnp.zeros((weights.shape[0], 2, 2, width), jnp.float32),
        jnp.zeros(head_w.shape, jnp.float32),
        jnp.zeros(head_b.shape, jnp.float32),
    )

    def advance(carry, item):
        terms = group_grads(item[0], item[1], weights, gains, biases, head_w, head_b, total)
        return (tuple((left + right for left, right in zip(carry, terms))), None)

    return lax.scan(advance, initial, (maps, labels))[0]


def per_device(images_in, labels, conv_weight, frn_gain, frn_bias, head_weight, head_bias):
    images = images_in.shape[0]
    width = frn_gain.shape[2]
    share = conv_weight.shape[3]
    total = images * lax.axis_size("dp") * lax.axis_size("section")
    offset = lax.axis_index("section") * share
    rounded_share = conv_weight.astype(jnp.bfloat16)
    all_conv = lax.all_gather(rounded_share, "section", axis=3, tiled=True)
    group_size = images // MICRO
    maps = images_in.reshape(MICRO, group_size, SIDE, SIDE, width)
    label_groups = labels.reshape(MICRO, group_size)
    conv_grad, norm_grad, head_w_grad, head_b_grad = accumulate(
        maps, label_groups, all_conv, frn_gain, frn_bias, head_weight, head_bias, total
    )
    summed = lax.psum(conv_grad, ("dp", "section"))
    conv_owned = lax.dynamic_slice_in_dim(summed, offset, share, 3)
    norm_sum, head_w_sum, head_b_sum = lax.psum(
        (norm_grad, head_w_grad, head_b_grad), ("dp", "section")
    )
    params = jnp.stack([frn_gain, frn_bias], axis=2)
    return (
        conv_owned + prior_precision * conv_weight,
        norm_sum + prior_precision * params,
        head_w_sum + prior_precision * head_weight,
        head_b_sum + prior_precision * head_bias,
    )


def solution(mesh):
    return jax.shard_map(
        per_device,
        mesh=mesh,
        in_specs=(
            P(("dp", "section"), None),
            P(("dp", "section")),
            P(None, None, None, "section"),
            P(),
            P(),
            P(),
            P(),
        ),
        out_specs=(P(None, None, None, "section"), P(), P(), P()),
        check_vma=False,
    )
```

profile of v0, /device:TPU:0, one launch (start us, length us, event | category | flops | bytes accessed | tf_op | source)
XLA Modules:
  0.0 816.5 jit_solution(12413973247500979296)
XLA Ops:
  9.6 8.5 %all_gather.3 = bf16[3,2,576,64]{2,3,1,0:T(8,128)(2,1)S(1)} all-gather(bf16[3,2,576,16]{2,3,1,0:T(8,128)(2,1)S(1)} %convert_element_type.386), channel_id=1, replica_groups=mesh['dp'=8,'section'=4] {'section'}, dimensions={3}, use_global_device_ids=true | all-gather | bytes 552960 | tf_op jit(solution)/shard_map/all_gather | solution.py:143
  19.2 659.0 %while.19 = (s32[]{:T(128)}, f32[3,2,576,64]{2,3,1,0:T(8,128)}, f32[3,2,2,64]{3,2,1,0:T(2,128)}, f32[64,10]{0,1:T(8,128)}, f32[10]{0:T(128)}, /*index=5*/bf16[8,...) while((s32[]{:T(128)}, f32[3,2,576,64]{2,3,1,0:T(8,128)}, ...), condition=%wide.region_29.30_spmd.clone, body=%wide.region_0.29_spmd.clone.sunk | while | flops 655682368 | bytes 99941760 | solution.py:133
  37.1 4.0 pad_slice_fusion.55
  56.0 4.0 pad_slice_fusion.57
  69.6 4.0 fusion.302
  119.4 4.0 pad_slice_fusion.55
  138.3 4.0 pad_slice_fusion.57
  152.0 4.0 fusion.302
  201.8 4.0 pad_slice_fusion.55
  220.7 4.0 pad_slice_fusion.57
  234.3 4.0 fusion.302
  284.2 4.0 pad_slice_fusion.55
  316.7 4.0 fusion.302
  366.5 4.0 pad_slice_fusion.55
  399.1 4.0 fusion.302
  448.9 4.0 pad_slice_fusion.55
  481.4 4.0 fusion.302
  531.3 4.0 pad_slice_fusion.55
  550.2 4.0 pad_slice_fusion.57
  563.8 4.0 fusion.302
  613.6 4.0 pad_slice_fusion.55
  646.1 4.0 fusion.302
  678.2 40.8 %all-reduce.51 = (f32[3,2,2,64]{3,2,1,0:T(2,128)S(1)}, f32[64,10]{0,1:T(8,128)S(1)}, f32[10]{0:T(128)S(1)}) all-reduce(f32[3,2,2,64]{3,2,1,0:T(2,128)} %get-tuple-element.157, f32[64,10]{0,1:T(8,128)} %get-tuple-element.158, f32[10]{0:T(128)} %get-tuple-element.159), channel_id=1, replica_groups=mesh['dp'=8,'section'=4] {'dp','section'}, use_global_device_ids=true, to_apply=%region_31.32 | all-reduce | flops 1418 | bytes 11344 | tf_op jit(solution)/shard_map/psum | solution.py:152
  722.8 85.1 %all-reduce.54.cloned.1.call-done = f32[3,2,576,64]{2,3,1,0:T(8,128)} async-done(((f32[3,2,576,64]{2,3,1,0:T(8,128)}), f32[3,2,576,64]{2,3,1,0:T(8,128)}) %all-reduce.54.cloned.1.call-update) | async-done | bytes 884752 | tf_op jit(solution)/shard_map/psum | solution.py:150
  (1667 shorter events, 581.6 us)
Async XLA Ops:
  7.2 800.7 %all-reduce.54.cloned.1.call-start = ((), (), s32[]{:S(2)}) async-start(), calls=%async_computation | async-start | bytes 1966080 | tf_op jit(solution)/shard_map/psum | solution.py:150
  19.2 23.2 %copy-start.5 = (bf16[3,2,576,64]{2,3,1,0:T(8,128)(2,1)}, bf16[3,2,576,64]{2,3,1,0:T(8,128)(2,1)S(1)}, u32[]{:S(2)}) copy-start(bf16[3,2,576,64]{2,3,1,0:T(8,128)(2,1)S(1)} %get-tuple-element.949) | copy-start | bytes 1327108 | tf_op jit(solution)/shard_map/while
  21.9 11.3 %copy-start.43 = (f32[64]{0:T(128)}, f32[64]{0:T(128)S(1)}, u32[]{:S(2)}) copy-start(f32[64]{0:T(128)S(1)} %get-tuple-element.737) | copy-start | bytes 772 | tf_op jit(solution)/shard_map/while
  21.9 20.9 %copy-start.40 = (f32[64]{0:T(128)}, f32[64]{0:T(128)S(1)}, u32[]{:S(2)}) copy-start(f32[64]{0:T(128)S(1)} %get-tuple-element.752) | copy-start | bytes 772 | tf_op jit(solution)/shard_map/while
  101.6 23.1 %copy-start.5 = (bf16[3,2,576,64]{2,3,1,0:T(8,128)(2,1)}, bf16[3,2,576,64]{2,3,1,0:T(8,128)(2,1)S(1)}, u32[]{:S(2)}) copy-start(bf16[3,2,576,64]{2,3,1,0:T(8,128)(2,1)S(1)} %get-tuple-element.949) | copy-start | bytes 1327108 | tf_op jit(solution)/shard_map/while
  104.2 11.3 %copy-start.43 = (f32[64]{0:T(128)}, f32[64]{0:T(128)S(1)}, u32[]{:S(2)}) copy-start(f32[64]{0:T(128)S(1)} %get-tuple-element.737) | copy-start | bytes 772 | tf_op jit(solution)/shard_map/while
  104.2 20.9 %copy-start.40 = (f32[64]{0:T(128)}, f32[64]{0:T(128)S(1)}, u32[]{:S(2)}) copy-start(f32[64]{0:T(128)S(1)} %get-tuple-element.752) | copy-start | bytes 772 | tf_op jit(solution)/shard_map/while
  184.0 23.1 %copy-start.5 = (bf16[3,2,576,64]{2,3,1,0:T(8,128)(2,1)}, bf16[3,2,576,64]{2,3,1,0:T(8,128)(2,1)S(1)}, u32[]{:S(2)}) copy-start(bf16[3,2,576,64]{2,3,1,0:T(8,128)(2,1)S(1)} %get-tuple-element.949) | copy-start | bytes 1327108 | tf_op jit(solution)/shard_map/while
  186.6 11.3 %copy-start.43 = (f32[64]{0:T(128)}, f32[64]{0:T(128)S(1)}, u32[]{:S(2)}) copy-start(f32[64]{0:T(128)S(1)} %get-tuple-element.737) | copy-start | bytes 772 | tf_op jit(solution)/shard_map/while
  186.6 20.9 %copy-start.40 = (f32[64]{0:T(128)}, f32[64]{0:T(128)S(1)}, u32[]{:S(2)}) copy-start(f32[64]{0:T(128)S(1)} %get-tuple-element.752) | copy-start | bytes 772 | tf_op jit(solution)/shard_map/while
  266.3 23.1 %copy-start.5 = (bf16[3,2,576,64]{2,3,1,0:T(8,128)(2,1)}, bf16[3,2,576,64]{2,3,1,0:T(8,128)(2,1)S(1)}, u32[]{:S(2)}) copy-start(bf16[3,2,576,64]{2,3,1,0:T(8,128)(2,1)S(1)} %get-tuple-element.949) | copy-start | bytes 1327108 | tf_op jit(solution)/shard_map/while
  268.9 11.3 %copy-start.43 = (f32[64]{0:T(128)}, f32[64]{0:T(128)S(1)}, u32[]{:S(2)}) copy-start(f32[64]{0:T(128)S(1)} %get-tuple-element.737) | copy-start | bytes 772 | tf_op jit(solution)/shard_map/while
  269.0 20.9 %copy-start.40 = (f32[64]{0:T(128)}, f32[64]{0:T(128)S(1)}, u32[]{:S(2)}) copy-start(f32[64]{0:T(128)S(1)} %get-tuple-element.752) | copy-start | bytes 772 | tf_op jit(solution)/shard_map/while
  348.7 23.1 %copy-start.5 = (bf16[3,2,576,64]{2,3,1,0:T(8,128)(2,1)}, bf16[3,2,576,64]{2,3,1,0:T(8,128)(2,1)S(1)}, u32[]{:S(2)}) copy-start(bf16[3,2,576,64]{2,3,1,0:T(8,128)(2,1)S(1)} %get-tuple-element.949) | copy-start | bytes 1327108 | tf_op jit(solution)/shard_map/while
  351.3 11.3 %copy-start.43 = (f32[64]{0:T(128)}, f32[64]{0:T(128)S(1)}, u32[]{:S(2)}) copy-start(f32[64]{0:T(128)S(1)} %get-tuple-element.737) | copy-start | bytes 772 | tf_op jit(solution)/shard_map/while
  351.3 20.9 %copy-start.40 = (f32[64]{0:T(128)}, f32[64]{0:T(128)S(1)}, u32[]{:S(2)}) copy-start(f32[64]{0:T(128)S(1)} %get-tuple-element.752) | copy-start | bytes 772 | tf_op jit(solution)/shard_map/while
  431.1 23.1 %copy-start.5 = (bf16[3,2,576,64]{2,3,1,0:T(8,128)(2,1)}, bf16[3,2,576,64]{2,3,1,0:T(8,128)(2,1)S(1)}, u32[]{:S(2)}) copy-start(bf16[3,2,576,64]{2,3,1,0:T(8,128)(2,1)S(1)} %get-tuple-element.949) | copy-start | bytes 1327108 | tf_op jit(solution)/shard_map/while
  433.7 11.3 %copy-start.43 = (f32[64]{0:T(128)}, f32[64]{0:T(128)S(1)}, u32[]{:S(2)}) copy-start(f32[64]{0:T(128)S(1)} %get-tuple-element.737) | copy-start | bytes 772 | tf_op jit(solution)/shard_map/while
  433.7 20.9 %copy-start.40 = (f32[64]{0:T(128)}, f32[64]{0:T(128)S(1)}, u32[]{:S(2)}) copy-start(f32[64]{0:T(128)S(1)} %get-tuple-element.752) | copy-start | bytes 772 | tf_op jit(solution)/shard_map/while
  513.4 23.1 %copy-start.5 = (bf16[3,2,576,64]{2,3,1,0:T(8,128)(2,1)}, bf16[3,2,576,64]{2,3,1,0:T(8,128)(2,1)S(1)}, u32[]{:S(2)}) copy-start(bf16[3,2,576,64]{2,3,1,0:T(8,128)(2,1)S(1)} %get-tuple-element.949) | copy-start | bytes 1327108 | tf_op jit(solution)/shard_map/while
  516.1 20.9 %copy-start.40 = (f32[64]{0:T(128)}, f32[64]{0:T(128)S(1)}, u32[]{:S(2)}) copy-start(f32[64]{0:T(128)S(1)} %get-tuple-element.752) | copy-start | bytes 772 | tf_op jit(solution)/shard_map/while
  595.8 23.1 %copy-start.5 = (bf16[3,2,576,64]{2,3,1,0:T(8,128)(2,1)}, bf16[3,2,576,64]{2,3,1,0:T(8,128)(2,1)S(1)}, u32[]{:S(2)}) copy-start(bf16[3,2,576,64]{2,3,1,0:T(8,128)(2,1)S(1)} %get-tuple-element.949) | copy-start | bytes 1327108 | tf_op jit(solution)/shard_map/while
  598.4 11.3 %copy-start.43 = (f32[64]{0:T(128)}, f32[64]{0:T(128)S(1)}, u32[]{:S(2)}) copy-start(f32[64]{0:T(128)S(1)} %get-tuple-element.737) | copy-start | bytes 772 | tf_op jit(solution)/shard_map/while
  598.4 20.9 %copy-start.40 = (f32[64]{0:T(128)}, f32[64]{0:T(128)S(1)}, u32[]{:S(2)}) copy-start(f32[64]{0:T(128)S(1)} %get-tuple-element.752) | copy-start | bytes 772 | tf_op jit(solution)/shard_map/while
  (378 other events, 790.3 us)
Sparse Core Ops, SparseCore 0:
  678.3 129.5 all-reduce.53
where the time goes:
time: 827 us; the launch traced here: 817 us
  local copies, waits for them, and re-layouts  424 us (51%)
  other arithmetic  151 us (18%)
  matrix products  85.6 us (10%)
  waiting for transfers between devices  85.1 us (10%)
  blocking collectives  49.3 us (6%)
  between operations  14.1 us (2%)
    concatenate x104, local copies, waits for them, and re-layouts, make_patches(): stacked = jnp.concatenate(taps, axis=3)  192 us
    slice x40, local copies, waits for them, and re-layouts, make_patches(): padded[:, a:a + side, e:e + side, :]  115 us
    psum x1, waiting for transfers between devices, per_device(): summed = lax.psum(conv_grad, ('dp', 'section'))  85.1 us
    while x800, local copies, waits for them, and re-layouts  72.5 us
    convert_element_type x40, other arithmetic, block_forward(): swish(skip + respond(pre_second, gains[1], biases[1], count))  48.6 us
    psum x1, blocking collectives, per_device(): lax.psum((norm_grad, head_w_grad, head_b_grad), ('dp', 'section'))  40.8 us
    convert_element_type x72, other arithmetic, block_forward(): swish(respond(pre_first, gains[0], biases[0], count)).astype(jnp.bfloat16)  37.2 us
    reduce_sum x48, other arithmetic, respond(): return (gain * normed + bias).reshape(values.shape)  36.8 us
  transfers between devices with their start and end apart: 1, of which 1 were waited for; matrix products, arithmetic and copies ran while one was open for 0% of the time, Pallas kernels for 0%

commit v1 on v0

--- a/solution.py
+++ b/solution.py
@@ -1,3 +1,4 @@
+import functools
 import jax
 import jax.numpy as jnp
 from jax import lax
@@ -7,6 +8,13 @@
 MICRO = 8
 eps = 1e-06
 prior_precision = 0.5
+
+
+def _time_spans(local_array, ax_name):
+    return jnp.sum(lax.all_gather(local_array, axis_name=ax_name), axis=0)
+
+
+launch_row_all = functools.partial(_time_spans, ax_name=("dp", "section"))
 
 
 def make_patches(maps):
@@ -147,7 +155,7 @@
     conv_grad, norm_grad, head_w_grad, head_b_grad = accumulate(
         maps, label_groups, all_conv, frn_gain, frn_bias, head_weight, head_bias, total
     )
-    summed = lax.psum(conv_grad, ("dp", "section"))
+    summed = launch_row_all(conv_grad)
     conv_owned = lax.dynamic_slice_in_dim(summed, offset, share, 3)
     norm_sum, head_w_sum, head_b_sum = lax.psum(
         (norm_grad, head_w_grad, head_b_grad), ("dp", "section")

time: 827 us -> 754 us (0.912)
  local copies, waits for them, and re-layouts: 424 us -> 287 us
  waiting for transfers between devices: 85.1 us -> 141 us
  matrix products: 85.6 us -> 94.8 us
    all_gather x0 -> x1, waiting for transfers between devices: none -> 141 us  [_time_spans(): return jnp.sum(lax.all_gather(local_array, axis_name=ax_name), axis=0)]
    psum x1 -> x0, waiting for transfers between devices: 85.1 us -> none  [per_device(): summed = lax.psum(conv_grad, ('dp', 'section'))]
    slice x40, local copies, waits for them, and re-layouts: 115 us -> 54.3 us  [make_patches(): padded[:, a:a + side, e:e + side, :]]
    concatenate x104, local copies, waits for them, and re-layouts: 192 us -> 144 us  [make_patches(): stacked = jnp.concatenate(taps, axis=3)]
    while x800 -> x1216, local copies, waits for them, and re-layouts: 72.5 us -> 43.8 us
    convert_element_type x72, other arithmetic: 37.2 us -> 11.4 us  [block_forward(): swish(respond(pre_first, gains[0], biases[0], count)).astype(jnp.bfloat16)]
    dot_general x24, matrix products: 6.28 us -> 22.4 us  [block_backward(): jnp.dot(cols_second.T, q_second, preferred_element_type=jnp.float32)]
    convert_element_type x40, other arithmetic: 48.6 us -> 33 us  [block_forward(): swish(skip + respond(pre_second, gains[1], biases[1], count))]
where the time goes in v1:
time: 754 us; the launch traced here: 746 us
  local copies, waits for them, and re-layouts  287 us (38%)
  other arithmetic  148 us (20%)
  waiting for transfers between devices  141 us (19%)
  matrix products  94.8 us (13%)
  blocking collectives  50.9 us (7%)
  between operations  14.1 us (2%)
  loops' own time  10.1 us (1%)
    concatenate x104, local copies, waits for them, and re-layouts, make_patches(): stacked = jnp.concatenate(taps, axis=3)  144 us
    all_gather x1, waiting for transfers between devices, _time_spans(): return jnp.sum(lax.all_gather(local_array, axis_name=ax_name), axis=0)  141 us
    slice x40, local copies, waits for them, and re-layouts, make_patches(): padded[:, a:a + side, e:e + side, :]  54.3 us
    reduce_sum x48, other arithmetic, respond(): return (gain * normed + bias).reshape(values.shape)  50.5 us
    while x1216, local copies, waits for them, and re-layouts  43.8 us
    psum x1, blocking collectives, per_device(): lax.psum((norm_grad, head_w_grad, head_b_grad), ('dp', 'section'))  42.4 us
    convert_element_type x40, other arithmetic, block_forward(): swish(skip + respond(pre_second, gains[1], biases[1], count))  33 us
    dot_general x24, matrix products, block_backward(): jnp.dot(cols_second.T, q_second, preferred_element_type=jnp.float32)  22.4 us
  transfers between devices with their start and end apart: 1, of which 1 were waited for; matrix products, arithmetic and copies ran while one was open for 0% of the time, Pallas kernels for 0%

profile of v1, /device:TPU:0, one launch (start us, length us, event | category | flops | bytes accessed | tf_op | source)
XLA Modules:
  0.0 745.8 jit_solution(737615511217034903)
XLA Ops:
  9.4 8.5 %all_gather.9 = bf16[3,2,576,64]{2,3,1,0:T(8,128)(2,1)S(1)} all-gather(bf16[3,2,576,16]{2,3,1,0:T(8,128)(2,1)S(1)} %convert_element_type.386), channel_id=1, replica_groups=mesh['dp'=8,'section'=4] {'section'}, dimensions={3}, use_global_device_ids=true | all-gather | bytes 552960 | tf_op jit(solution)/shard_map/all_gather | solution.py:151
  18.6 521.4 %while.19 = (s32[]{:T(128)}, f32[3,2,576,64]{2,3,1,0:T(8,128)}, f32[3,2,2,64]{3,2,1,0:T(2,128)}, f32[64,10]{0,1:T(8,128)}, f32[10]{0:T(128)}, /*index=5*/bf16[8,...) while((s32[]{:T(128)}, f32[3,2,576,64]{2,3,1,0:T(8,128)}, ...), condition=%wide.region_29.30_spmd.clone, body=%wide.region_0.29_spmd.clone.sunk | while | flops 655682368 | bytes 94042408 | solution.py:141
  41.0 2.2 concatenate.404
  62.9 2.3 multiply_reduce_fusion.38
  106.1 2.2 concatenate.404
  108.3 2.1 concatenate.405
  128.1 2.3 multiply_reduce_fusion.38
  171.3 2.2 concatenate.404
  193.3 2.3 multiply_reduce_fusion.38
  236.5 2.2 concatenate.404
  238.7 2.1 concatenate.405
  258.5 2.3 multiply_reduce_fusion.38
  301.7 2.2 concatenate.404
  303.9 2.1 concatenate.405
  323.6 2.3 multiply_reduce_fusion.38
  366.9 2.2 concatenate.404
  388.8 2.3 multiply_reduce_fusion.38
  432.0 2.2 concatenate.404
  454.0 2.3 multiply_reduce_fusion.38
  497.2 2.2 concatenate.404
  519.2 2.3 multiply_reduce_fusion.38
  540.0 42.4 %all-reduce.51 = (f32[3,2,2,64]{3,2,1,0:T(2,128)S(1)}, f32[64,10]{0,1:T(8,128)S(1)}, f32[10]{0:T(128)S(1)}) all-reduce(f32[3,2,2,64]{3,2,1,0:T(2,128)} %get-tuple-element.962, f32[64,10]{0,1:T(8,128)} %get-tuple-element.963, f32[10]{0:T(128)} %get-tuple-element.964), channel_id=1, replica_groups=mesh['dp'=8,'section'=4] {'dp','section'}, use_global_device_ids=true, to_apply=%region_31.32 | all-reduce | flops 1418 | bytes 11344 | tf_op jit(solution)/shard_map/psum | solution.py:160
  585.5 141.4 %all-gather.3.cloned.1.call-done = f32[96,2,576,64]{2,3,1,0:T(8,128)} async-done(((f32[3,2,576,64]{2,3,1,0:T(8,128)}), f32[96,2,576,64]{2,3,1,0:T(8,128)}) %all-gather.3.cloned.1.call-update) | async-done | bytes 28311568 | tf_op jit(solution)/shard_map/all_gather | solution.py:14
  726.9 11.4 %reduce_sum.441 = f32[3,2,576,64]{2,3,1,0:T(8,128)S(1)} reduce(f32[32,3,2,576,64]{3,4,2,1,0:T(8,128)} %bitcast.784, f32[]{:T(128)} %constant.108.clone.1), dimensions={0}, to_apply=%region_30.31 | reduce | flops 6856704 | bytes 29196292 | tf_op jit(solution)/shard_map/reduce_sum | solution.py:14
  (2090 shorter events, 476.0 us)
Async XLA Ops:
  7.2 719.7 %all-gather.3.cloned.1.call-start = ((), (), s32[]{:S(2)}) async-start(), calls=%async_computation | async-start | bytes 32440320 | tf_op jit(solution)/shard_map/all_gather | solution.py:14
  20.3 28.8 %copy-start.43 = (f32[64]{0:T(128)}, f32[64]{0:T(128)S(1)}, u32[]{:S(2)}) copy-start(f32[64]{0:T(128)S(1)} %get-tuple-element.799) | copy-start | bytes 772 | tf_op jit(solution)/shard_map/while
  20.3 28.8 %copy-start.45 = (f32[64]{0:T(128)}, f32[64]{0:T(128)S(1)}, u32[]{:S(2)}) copy-start(f32[64]{0:T(128)S(1)} %get-tuple-element.800) | copy-start | bytes 772 | tf_op jit(solution)/shard_map/while
  83.7 26.8 %copy-start.3 = (bf16[3,2,576,64]{2,3,1,0:T(8,128)(2,1)}, bf16[3,2,576,64]{2,3,1,0:T(8,128)(2,1)S(1)}, u32[]{:S(2)}) copy-start(bf16[3,2,576,64]{2,3,1,0:T(8,128)(2,1)S(1)} %get-tuple-element.949) | copy-start | bytes 1327108 | tf_op jit(solution)/shard_map/while
  85.5 28.8 %copy-start.43 = (f32[64]{0:T(128)}, f32[64]{0:T(128)S(1)}, u32[]{:S(2)}) copy-start(f32[64]{0:T(128)S(1)} %get-tuple-element.799) | copy-start | bytes 772 | tf_op jit(solution)/shard_map/while
  85.5 28.8 %copy-start.45 = (f32[64]{0:T(128)}, f32[64]{0:T(128)S(1)}, u32[]{:S(2)}) copy-start(f32[64]{0:T(128)S(1)} %get-tuple-element.800) | copy-start | bytes 772 | tf_op jit(solution)/shard_map/while
  148.9 26.8 %copy-start.3 = (bf16[3,2,576,64]{2,3,1,0:T(8,128)(2,1)}, bf16[3,2,576,64]{2,3,1,0:T(8,128)(2,1)S(1)}, u32[]{:S(2)}) copy-start(bf16[3,2,576,64]{2,3,1,0:T(8,128)(2,1)S(1)} %get-tuple-element.949) | copy-start | bytes 1327108 | tf_op jit(solution)/shard_map/while
  150.7 28.8 %copy-start.43 = (f32[64]{0:T(128)}, f32[64]{0:T(128)S(1)}, u32[]{:S(2)}) copy-start(f32[64]{0:T(128)S(1)} %get-tuple-element.799) | copy-start | bytes 772 | tf_op jit(solution)/shard_map/while
  150.7 28.8 %copy-start.45 = (f32[64]{0:T(128)}, f32[64]{0:T(128)S(1)}, u32[]{:S(2)}) copy-start(f32[64]{0:T(128)S(1)} %get-tuple-element.800) | copy-start | bytes 772 | tf_op jit(solution)/shard_map/while
  214.1 26.8 %copy-start.3 = (bf16[3,2,576,64]{2,3,1,0:T(8,128)(2,1)}, bf16[3,2,576,64]{2,3,1,0:T(8,128)(2,1)S(1)}, u32[]{:S(2)}) copy-start(bf16[3,2,576,64]{2,3,1,0:T(8,128)(2,1)S(1)} %get-tuple-element.949) | copy-start | bytes 1327108 | tf_op jit(solution)/shard_map/while
  215.9 28.8 %copy-start.43 = (f32[64]{0:T(128)}, f32[64]{0:T(128)S(1)}, u32[]{:S(2)}) copy-start(f32[64]{0:T(128)S(1)} %get-tuple-element.799) | copy-start | bytes 772 | tf_op jit(solution)/shard_map/while
  215.9 28.8 %copy-start.45 = (f32[64]{0:T(128)}, f32[64]{0:T(128)S(1)}, u32[]{:S(2)}) copy-start(f32[64]{0:T(128)S(1)} %get-tuple-element.800) | copy-start | bytes 772 | tf_op jit(solution)/shard_map/while
  279.2 26.8 %copy-start.3 = (bf16[3,2,576,64]{2,3,1,0:T(8,128)(2,1)}, bf16[3,2,576,64]{2,3,1,0:T(8,128)(2,1)S(1)}, u32[]{:S(2)}) copy-start(bf16[3,2,576,64]{2,3,1,0:T(8,128)(2,1)S(1)} %get-tuple-element.949) | copy-start | bytes 1327108 | tf_op jit(solution)/shard_map/while
  281.1 28.8 %copy-start.43 = (f32[64]{0:T(128)}, f32[64]{0:T(128)S(1)}, u32[]{:S(2)}) copy-start(f32[64]{0:T(128)S(1)} %get-tuple-element.799) | copy-start | bytes 772 | tf_op jit(solution)/shard_map/while
  281.1 28.8 %copy-start.45 = (f32[64]{0:T(128)}, f32[64]{0:T(128)S(1)}, u32[]{:S(2)}) copy-start(f32[64]{0:T(128)S(1)} %get-tuple-element.800) | copy-start | bytes 772 | tf_op jit(solution)/shard_map/while
  344.4 26.8 %copy-start.3 = (bf16[3,2,576,64]{2,3,1,0:T(8,128)(2,1)}, bf16[3,2,576,64]{2,3,1,0:T(8,128)(2,1)S(1)}, u32[]{:S(2)}) copy-start(bf16[3,2,576,64]{2,3,1,0:T(8,128)(2,1)S(1)} %get-tuple-element.949) | copy-start | bytes 1327108 | tf_op jit(solution)/shard_map/while
  346.2 28.8 %copy-start.43 = (f32[64]{0:T(128)}, f32[64]{0:T(128)S(1)}, u32[]{:S(2)}) copy-start(f32[64]{0:T(128)S(1)} %get-tuple-element.799) | copy-start | bytes 772 | tf_op jit(solution)/shard_map/while
  346.2 28.8 %copy-start.45 = (f32[64]{0:T(128)}, f32[64]{0:T(128)S(1)}, u32[]{:S(2)}) copy-start(f32[64]{0:T(128)S(1)} %get-tuple-element.800) | copy-start | bytes 772 | tf_op jit(solution)/shard_map/while
  409.6 26.8 %copy-start.3 = (bf16[3,2,576,64]{2,3,1,0:T(8,128)(2,1)}, bf16[3,2,576,64]{2,3,1,0:T(8,128)(2,1)S(1)}, u32[]{:S(2)}) copy-start(bf16[3,2,576,64]{2,3,1,0:T(8,128)(2,1)S(1)} %get-tuple-element.949) | copy-start | bytes 1327108 | tf_op jit(solution)/shard_map/while
  411.4 28.8 %copy-start.43 = (f32[64]{0:T(128)}, f32[64]{0:T(128)S(1)}, u32[]{:S(2)}) copy-start(f32[64]{0:T(128)S(1)} %get-tuple-element.799) | copy-start | bytes 772 | tf_op jit(solution)/shard_map/while
  411.4 28.8 %copy-start.45 = (f32[64]{0:T(128)}, f32[64]{0:T(128)S(1)}, u32[]{:S(2)}) copy-start(f32[64]{0:T(128)S(1)} %get-tuple-element.800) | copy-start | bytes 772 | tf_op jit(solution)/shard_map/while
  474.8 26.8 %copy-start.3 = (bf16[3,2,576,64]{2,3,1,0:T(8,128)(2,1)}, bf16[3,2,576,64]{2,3,1,0:T(8,128)(2,1)S(1)}, u32[]{:S(2)}) copy-start(bf16[3,2,576,64]{2,3,1,0:T(8,128)(2,1)S(1)} %get-tuple-element.949) | copy-start | bytes 1327108 | tf_op jit(solution)/shard_map/while
  476.6 28.8 %copy-start.43 = (f32[64]{0:T(128)}, f32[64]{0:T(128)S(1)}, u32[]{:S(2)}) copy-start(f32[64]{0:T(128)S(1)} %get-tuple-element.799) | copy-start | bytes 772 | tf_op jit(solution)/shard_map/while
  476.6 28.8 %copy-start.45 = (f32[64]{0:T(128)}, f32[64]{0:T(128)S(1)}, u32[]{:S(2)}) copy-start(f32[64]{0:T(128)S(1)} %get-tuple-element.800) | copy-start | bytes 772 | tf_op jit(solution)/shard_map/while
  (589 other events, 1426.4 us)
Sparse Core Ops, SparseCore 0:
  540.1 186.7 all-gather.2
